TPU v7x, 256 devices: a whole 4x4x8 slice. The times are simulated.
256 devices in a mesh: row: 8 (over x_lo, y), col: 32 (over z, x_hi, core).
Axes of the slice: x: 4 (x_hi: 2, x_lo: 2; x = x_hi * 2 + x_lo), y: 4, z: 8, core: 2. Of those that a mesh axis runs over, the one named last changes fastest.
Arguments:
- tile_values: bfloat16 [8, 32, 32, 3, 128, 128], P('row', 'col'), may hold values from -6 to 6
- tile_slots: int32 [8, 32, 32, 3, 3], P('row', 'col'), may hold values from 0 to 59, as said below
- counts: int32 [8, 32, 32], P('row', 'col'), may hold values from 1 to 3, as said below
- factor: bfloat16 [32768, 128], P(('row', 'col'))
- d_factor: bfloat16 [32768, 128], P(('row', 'col'))
- core_rel: bfloat16 [60, 128, 128], replicated, may hold values from -0.5 to 0.5
- d_core: bfloat16 [60, 128, 128], replicated, may hold values from -0.5 to 0.5
Outputs:
- hv_factor: bfloat16 [32768, 128], P(('row', 'col'))
- hv_core: float32 [60, 128, 128], replicated
Inputs may be any that keep to these rules, and one draw needn't show every extreme that they name: `counts`: every device has, for every row span, at least one live slot, and in every draw some row span of every device has exactly 3 live slots. `tile_slots`: the three entries of a slot are a relation below 60, a row tile that is always 0 (each row span is one tile) and a column tile below 8; dead slots hold such entries too.
All inputs are finite; a program needn't handle non-finite values.
Results may differ from a plain program's by a relative error of at most 0.002.
The roundings to bfloat16 on the way count: a program that leaves them out, or rounds other values in their place, can miss the bound.
Values may be sent and summed in bfloat16 or wider, within the bound.
No kernel may reach another device: no remote copies, remote signals or barrier semaphores. Data moves between devices by JAX's collectives and lax.ppermute only.
A program may use at most 128 MiB of HBM per device.

v0:
```python
import jax
import jax.numpy as jnp
from jax import lax
from jax.sharding import PartitionSpec as P

HIGH = lax.Precision.HIGHEST


def core_direction(gram, d_gram, core_rel, d_core, core_sum):
    relation = core_rel.astype(jnp.float32)
    d_relation = d_core.astype(jnp.float32)
    left = jnp.einsum("ab,kbc->kac", d_gram, relation, precision=HIGH) + jnp.einsum(
        "ab,kbc->kac", gram, d_relation, precision=HIGH
    )
    right = jnp.einsum("ab,kbc->kac", gram, relation, precision=HIGH)
    result = jnp.einsum("kac,cd->kad", left, gram, precision=HIGH) + jnp.einsum(
        "kac,cd->kad", right, d_gram, precision=HIGH
    )
    return result - core_sum


def per_device(tile_values, tile_slots, counts, factor, d_factor, core_rel, d_core):
    rank = factor.shape[1]
    span_rows = factor.shape[0]
    groups = tile_values.shape[2]
    capacity = tile_values.shape[3]
    tile_width = tile_values.shape[4]
    relations = core_rel.shape[0]
    slot_count = groups * capacity
    per_span = span_rows // tile_width
    pair = jnp.concatenate([d_factor, factor], axis=1)
    gram_local = jnp.einsum("na,nb->ab", factor, factor, preferred_element_type=jnp.float32)
    cross_local = jnp.einsum("na,nb->ab", factor, d_factor, preferred_element_type=jnp.float32)
    gram, cross = lax.psum((gram_local, cross_local), ("row", "col"))
    column_block = lax.all_gather(pair, "row", axis=0, tiled=True)
    row_block = lax.all_gather(pair, "col", axis=0, tiled=True)
    block = tile_values.reshape(slot_count, tile_width, tile_width)
    index = tile_slots.reshape(slot_count, 3)
    live = (jnp.arange(capacity, dtype=jnp.int32)[None, :] < counts.reshape(groups, 1)).reshape(
        slot_count
    )
    block = jnp.where(live[:, None, None], block, jnp.zeros_like(block))
    group_ids = jnp.repeat(jnp.arange(groups, dtype=jnp.int32), capacity)
    row_tiles = row_block.reshape(-1, tile_width, 2 * rank)
    column_tiles = column_block.reshape(-1, tile_width, 2 * rank)
    rows_fac = jnp.take(row_tiles, group_ids * per_span + index[:, 1], axis=0)
    cols_fac = jnp.take(column_tiles, index[:, 2], axis=0)
    near = jnp.einsum("suv,svc->suc", block, cols_fac, preferred_element_type=jnp.float32).astype(
        jnp.bfloat16
    )
    far = jnp.einsum("suv,suc->svc", block, rows_fac, preferred_element_type=jnp.float32).astype(
        jnp.bfloat16
    )
    rel_pick = jnp.take(core_rel, index[:, 0], axis=0)
    d_rel_pick = jnp.take(d_core, index[:, 0], axis=0)
    row_term = jnp.einsum(
        "suq,srq->sur", near[..., :rank], rel_pick, preferred_element_type=jnp.float32
    ) + jnp.einsum("suq,srq->sur", near[..., rank:], d_rel_pick, preferred_element_type=jnp.float32)
    col_term = jnp.einsum(
        "svq,sqr->svr", far[..., :rank], rel_pick, preferred_element_type=jnp.float32
    ) + jnp.einsum("svq,sqr->svr", far[..., rank:], d_rel_pick, preferred_element_type=jnp.float32)
    core_slot = jnp.einsum(
        "sua,sub->sab", rows_fac[..., rank:], near[..., :rank], preferred_element_type=jnp.float32
    ) + jnp.einsum(
        "sua,sub->sab", rows_fac[..., :rank], near[..., rank:], preferred_element_type=jnp.float32
    )
    row_onehot = (
        index[:, 1].reshape(groups, capacity, 1)
        == jnp.arange(per_span, dtype=jnp.int32)[None, None, :]
    ).astype(jnp.float32)
    row_place = jnp.einsum(
        "gck,gcud->gkud",
        row_onehot,
        row_term.reshape(groups, capacity, tile_width, rank),
        precision=HIGH,
    ).reshape(-1, rank)
    col_onehot = (
        index[:, 2][:, None] == jnp.arange(column_tiles.shape[0], dtype=jnp.int32)[None, :]
    ).astype(jnp.float32)
    col_place = jnp.einsum("sk,svd->kvd", col_onehot, col_term, precision=HIGH).reshape(-1, rank)
    rel_onehot = (jnp.arange(relations, dtype=jnp.int32)[:, None] == index[:, 0][None, :]).astype(
        jnp.float32
    )
    core_local = jnp.einsum("ks,sab->kab", rel_onehot, core_slot, precision=HIGH)
    row_shares = lax.psum_scatter(row_place, "col", scatter_dimension=0, tiled=True)
    col_shares = lax.psum_scatter(col_place, "row", scatter_dimension=0, tiled=True)
    hv_factor = (-(row_shares + col_shares)).astype(jnp.bfloat16)
    core_sum = lax.psum(core_local, ("row", "col"))
    d_gram = cross + cross.T
    hv_core = core_direction(gram, d_gram, core_rel, d_core, core_sum)
    return (hv_factor, hv_core)


def solution(mesh):
    placed = (
        P("row", "col", None, None, None, None),
        P("row", "col", None, None, None),
        P("row", "col", None),
        P(("row", "col"), None),
        P(("row", "col"), None),
        P(),
        P(),
    )
    return jax.shard_map(
        per_device,
        mesh=mesh,
        in_specs=placed,
        out_specs=(P(("row", "col"), None), P()),
        check_vma=False,
    )
```

profile of v0, /device:TPU:2, one launch (start us, length us, event | category | flops | bytes accessed | tf_op | source)
XLA Modules:
  0.0 556.2 jit_solution(6304980659275406926)
XLA Ops:
  10.6 4.6 copy.15
  15.5 4.2 gather_fusion.3
  22.6 29.1 %all_gather.6 = bf16[1024,256]{1,0:T(8,128)(2,1)S(1)} all-gather(bf16[128,256]{1,0:T(8,128)(2,1)S(1)} %copy-done.14), channel_id=1, replica_groups=mesh['row'=8,'col'=32] {'row'}, dimensions={0}, use_global_device_ids=true | all-gather | bytes 589824 | tf_op jit(solution)/shard_map/all_gather | solution.py:35
  51.7 5.9 %gather_fusion = bf16[96,128,256]{2,1,0:T(8,128)(2,1)} fusion(bf16[8,128,256]{2,1,0:T(8,128)(2,1)S(1)} %bitcast.71, s32[1024]{0:T(1024)S(1)} %get-tuple-element.16), kind=kCustom, calls=%fused_computation.2 | custom fusion | bytes 12583296 | tf_op jit(solution)/shard_map/jit(_take)/gather | solution.py:47
  57.6 8.7 %fusion.14 = bf16[96,128,256]{2,1,0:T(8,128)(2,1)} fusion(bf16[96,128,256]{2,1,0:T(8,128)(2,1)} %gather_fusion, pred[96]{0:T(512)(128)(4,1)S(1)} %get-tuple-element.13, bf16[96,128,128]{1,2,0:T(8,128)(2,1)} %copy.15, pred[96]{0:T(512)(128)(4,1)S(1)} %lt.48), kind=kOutput, calls=%fused_computation.23 | convolution fusion | flops 813170688 | bytes 15728832 | tf_op jit(solution)/shard_map/suv,svc->suc/dot_general | solution.py:48
  66.3 4.4 fusion.27
  70.8 4.1 fusion.32
  74.8 11.5 %fusion = f32[32,1,128,128]{3,1,2,0:T(1,128)} fusion(pred[32,3,1,1]{1,2,3,0:T(4,128)(4,1)S(1)} %reshape.122, f32[32,3,128,128]{3,2,1,0:T(8,128)S(1)} %bitcast.72), kind=kOutput, calls=%fused_computation.4 | convolution fusion | flops 18874368 | bytes 8388704 | tf_op jit(solution)/shard_map/gck,gcud->gkud/dot_general | solution.py:71
  88.1 4.8 all-gather.2.cloned.1.call-done
  92.9 7.8 %gather_fusion.1 = bf16[96,128,256]{2,1,0:T(8,128)(2,1)} fusion(bf16[32,128,256]{2,1,0:T(8,128)(2,1)} %bitcast.75, s32[1024]{0:T(1024)S(1)} %pad_clamp_fusion), kind=kCustom, calls=%fused_computation.3 | custom fusion | bytes 12583296 | tf_op jit(solution)/shard_map/jit(_take)/gather | solution.py:46
  100.7 3.4 broadcast_select_fusion
  104.1 6.1 %convolution_convert_fusion = bf16[96,128,256]{2,1,0:T(8,128)(2,1)S(1)} fusion(bf16[96,128,256]{2,1,0:T(8,128)(2,1)S(1)} %broadcast_select_fusion, bf16[96,128,128]{1,2,0:T(8,128)(2,1)} %copy.15, pred[96]{0:T(512)(128)(4,1)S(1)} %lt.48), kind=kOutput, calls=%fused_computation.22 | convolution fusion | flops 810024960 | bytes 15728736 | tf_op jit(solution)/shard_map/suv,suc->svc/dot_general | solution.py:51
  113.2 21.9 %fusion.4 = f32[8,128,128]{2,0,1:T(8,128)S(1)} fusion(f32[96,128,128]{2,1,0:T(8,128)S(1)} %fusion.21, f32[96,128,128]{2,1,0:T(8,128)S(1)} %fusion.23, s32[96]{0:T(128)S(1)} %get-tuple-element.12), kind=kOutput, calls=%fused_computation.10 | convolution fusion | flops 152568576 | bytes 13107584 | tf_op jit(solution)/shard_map/sk,svd->kvd/dot_general | solution.py:80
  136.1 3.8 fusion.17
  139.9 4.0 fusion.19
  144.0 13.9 %fusion.2 = f32[60,128,128]{2,0,1:T(8,128)S(1)} fusion(f32[96,128,128]{2,1,0:T(8,128)} %fusion.17, f32[96,128,128]{2,1,0:T(8,128)S(1)} %fusion.19, s32[96]{0:T(128)S(1)} %get-tuple-element.10), kind=kOutput, calls=%fused_computation.7 | convolution fusion | flops 1134040704 | bytes 16515456 | tf_op jit(solution)/shard_map/ks,sab->kab/dot_general | solution.py:84
  157.8 4.2 copy.19
  162.1 50.8 %reduce-scatter.3.cloned.1.call-done = f32[128,128]{1,0:T(8,128)} async-done(((f32[4096,128]{1,0:T(8,128)}), f32[128,128]{1,0:T(8,128)}) %reduce-scatter.3.cloned.1.call-update) | async-done | bytes 65552 | tf_op jit(solution)/shard_map/reduce_scatter | solution.py:85
  212.9 40.9 %reduce-scatter.5.cloned.1.call-done = f32[128,128]{1,0:T(8,128)} async-done(((f32[1024,128]{1,0:T(8,128)}), f32[128,128]{1,0:T(8,128)}) %reduce-scatter.5.cloned.1.call-update) | async-done | bytes 65552 | tf_op jit(solution)/shard_map/reduce_scatter | solution.py:86
  255.3 274.4 %all-reduce.3.cloned.1.call-done = (f32[60,128,128]{2,1,0:T(8,128)}, f32[128,128]{1,0:T(8,128)}, f32[128,128]{1,0:T(8,128)}) async-done(((f32[60,128,128]{2,1,0:T(8,128)}, f32[128,128]{1,0:T(8,128)}, f32[128,128]{1,0:T(8,128)}), (f32[60,128,128]{2,1,0:T(8,128)}, f32[128,128]{1,0:T(8,128)}, f32[128,128]{1,0:T(8,128)})) %all-reduce.3.cloned.1.call-update) | async-done | bytes 4063248 | tf_op jit(solution)/shard_map/psum | solution.py:88
  529.8 4.6 fusion.37
  534.4 3.7 fusion.40
  540.3 3.4 fusion.9
  543.7 5.5 add_subtract_fusion
  (70 shorter events, 15.8 us)
Async XLA Ops:
  7.2 12.6 %copy-start = (bf16[60,128,128]{2,1,0:T(8,128)(2,1)S(1)}, bf16[60,128,128]{2,1,0:T(8,128)(2,1)}, u32[]{:S(2)}) copy-start(bf16[60,128,128]{2,1,0:T(8,128)(2,1)} %param.14) | copy-start | bytes 5898244
  7.2 8.1 %copy-start.16 = (s32[1,1,32]{2,1,0:T(1,128)S(1)}, s32[1,1,32]{2,1,0:T(1,128)}, u32[]{:S(2)}) copy-start(s32[1,1,32]{2,1,0:T(1,128)} %param.11) | copy-start | bytes 388
  7.2 85.7 %all-gather.2.cloned.1.call-start = ((), (), s32[]{:S(2)}) async-start(), calls=%async_computation.3 | async-start | bytes 2162688 | tf_op jit(solution)/shard_map/all_gather | solution.py:36
  8.9 0.6 copy-start.13
  9.5 203.4 %reduce-scatter.3.cloned.1.call-start = ((), (), s32[]{:S(2)}) async-start(), calls=%async_computation.2 | async-start | bytes 2162688 | tf_op jit(solution)/shard_map/reduce_scatter | solution.py:85
  19.7 2.8 copy-start.14
  57.6 8.7 %copy-start.2 = (bf16[96,128,128]{2,1,0:T(8,128)(2,1)S(1)}, bf16[96,128,128]{2,1,0:T(8,128)(2,1)}, u32[]{:S(2)}) copy-start(bf16[96,128,128]{2,1,0:T(8,128)(2,1)} %gather_fusion.3) | copy-start | bytes 9437188
  66.3 4.4 copy-start.4
  74.8 11.6 %copy-start.12 = (bf16[128,128]{1,0:T(8,128)(2,1)S(1)}, bf16[128,128]{1,0:T(8,128)(2,1)}, u32[]{:S(2)}) copy-start(bf16[128,128]{1,0:T(8,128)(2,1)} %param.12) | copy-start | bytes 98308
  74.8 11.6 %copy-start.15 = (bf16[128,128]{1,0:T(8,128)(2,1)S(1)}, bf16[128,128]{1,0:T(8,128)(2,1)}, u32[]{:S(2)}) copy-start(bf16[128,128]{1,0:T(8,128)(2,1)} %param.13) | copy-start | bytes 98308
  86.4 167.5 %reduce-scatter.5.cloned.1.call-start = ((), (), s32[]{:S(2)}) async-start(), calls=%async_computation.4 | async-start | bytes 589824 | tf_op jit(solution)/shard_map/reduce_scatter | solution.py:86
  104.1 32.0 %copy-start.1 = (bf16[96,128,256]{2,1,0:T(8,128)(2,1)}, bf16[96,128,256]{2,1,0:T(8,128)(2,1)S(1)}, u32[]{:S(2)}) copy-start(bf16[96,128,256]{2,1,0:T(8,128)(2,1)S(1)} %broadcast_select_fusion) | copy-start | bytes 18874372
  104.1 6.1 %copy-start.3 = (bf16[96,128,128]{2,1,0:T(8,128)(2,1)S(1)}, bf16[96,128,128]{2,1,0:T(8,128)(2,1)}, u32[]{:S(2)}) copy-start(bf16[96,128,128]{2,1,0:T(8,128)(2,1)} %gather_fusion.3) | copy-start | bytes 9437188
  110.2 1.9 copy-start.5
  112.2 23.9 %slice-start = ((s8[6291456]{0:T(1024)(128)(4,1)}), s8[2097152]{0:T(1024)(128)(4,1)S(1)}, s32[]{:S(2)}) async-start(s8[6291456]{0:T(1024)(128)(4,1)} %bitcast.73), calls=%async_computation.6 | async-start | bytes 4194304
  113.2 22.8 %slice-start.1 = ((s8[6291456]{0:T(1024)(128)(4,1)}), s8[4194304]{0:T(1024)(128)(4,1)S(1)}, s32[]{:S(2)}) async-start(s8[6291456]{0:T(1024)(128)(4,1)} %bitcast.73), calls=%async_computation.7 | async-start | bytes 8388608
  139.9 389.9 %all-reduce.3.cloned.1.call-start = ((), (), s32[]{:S(2)}) async-start(), calls=%async_computation.5 | async-start | bytes 8126464 | tf_op jit(solution)/shard_map/psum | solution.py:88
  529.8 4.6 copy-start.8
  529.8 4.6 copy-start.10
  534.4 3.7 copy-start.11
  538.2 2.1 copy-start.7
  540.3 3.4 copy-start.6
  540.3 3.4 copy-start.9
Sparse Core Ops, SparseCore 0:
  10.8 82.0 all-gather.1
  97.0 115.8 reduce-scatter.2
  215.6 38.2 reduce-scatter.4
  260.1 269.6 all-reduce.2
where the time goes:
time: 567 us; the launch traced here: 556 us
  waiting for transfers between devices  371 us (65%)
  matrix products  101 us (18%)
  local copies, waits for them, and re-layouts  35.2 us (6%)
  blocking collectives  29.1 us (5%)
  between operations  14.5 us (3%)
    psum x1, waiting for transfers between devices, per_device(): core_sum = lax.psum(core_local, ('row', 'col'))  274 us
    reduce_scatter x1, waiting for transfers between devices, per_device(): lax.psum_scatter(row_place, 'col', scatter_dimension=0, tiled=True)  50.8 us
    reduce_scatter x1, waiting for transfers between devices, per_device(): lax.psum_scatter(col_place, 'row', scatter_dimension=0, tiled=True)  40.9 us
    all_gather x1, blocking collectives, per_device(): column_block = lax.all_gather(pair, 'row', axis=0, tiled=True)  29.1 us
    dot_general x1, matrix products, per_device(): jnp.einsum('sk,svd->kvd', col_onehot, col_term, precision=HIGH)  21.9 us
    dot_general x1, matrix products, per_device(): jnp.einsum('ks,sab->kab', rel_onehot, core_slot, precision=HIGH)  13.9 us
    dot_general x1, matrix products, per_device(): jnp.einsum('gck,gcud->gkud', row_onehot, row_term.reshape(groups, capacit...  11.5 us
  transfers between devices with their start and end apart: 4, of which 4 were waited for; matrix products, arithmetic and copies ran while one was open for 21% of the time, Pallas kernels for 0%

commit v1 on v0

v1 whole, which is shorter than its diff:
```python
import jax
import jax.numpy as jnp
from jax import lax
from jax.experimental import pallas as pl
from jax.experimental.pallas import tpu as pltpu
from jax.sharding import Mesh
from jax.sharding import PartitionSpec as P

F32 = jnp.float32
BF16 = jnp.bfloat16
I16 = jnp.int16
I32 = jnp.int32
HIGH = lax.Precision.HIGHEST

T = 128
SC = 3
NR = 8
NQ = 16
RELS = 60
HALF = RELS // 2 * T
PART = HALF // NR
PIECE = 32
GRP = 160
NGRP = HALF // GRP
SEND_CORE = NQ * T
SEND_EXP = SEND_CORE + HALF
SEND_ROWS = SEND_EXP + 48
C1_CORE = T
C1_GRAM = C1_CORE + PART
C1_EXP = C1_GRAM + 32
C1_ROWS = C1_EXP + 16
C2_CORE = T
C2_GRAM = C2_CORE + PIECE
C2_EXP = C2_GRAM + 32
C2_ROWS = C2_EXP + 16
P3_ROWS = PIECE + 16
P4_ROWS = PART + 16

NT = (((1,), (1,)), ((), ()))
TN = (((0,), (0,)), ((), ()))


def exponent_of(x):
    top = jnp.max(jnp.abs(x), axis=0, keepdims=True)
    e = jnp.floor(jnp.log2(jnp.maximum(top, 1e-37))) + 1.0
    return jnp.clip(e, -100.0, 127.0)


def coded(x, e):
    q = jnp.round(x * jnp.exp2(15.0 - e))
    return jnp.clip(q, -32767.0, 32767.0).astype(I32)


def enc(x):
    e = exponent_of(x)
    return coded(x, e).astype(I16), e


def enc_wide(x):
    e = exponent_of(x)
    q = x * jnp.exp2(15.0 - e)
    hi = jnp.clip(jnp.round(q), -32767.0, 32767.0)
    lo = jnp.clip(jnp.round((q - hi) * 16384.0), -32767.0, 32767.0)
    return hi.astype(I32).astype(I16), lo.astype(I32).astype(I16), e


def dec(q, e):
    return q.astype(I32).astype(F32) * jnp.exp2(e - 15.0)


def dec_wide(hi, lo, e):
    return (hi.astype(I32).astype(F32) + lo.astype(I32).astype(F32) * (1.0 / 16384.0)) * jnp.exp2(e - 15.0)


def exps_of(block):
    return block.astype(I32).astype(F32)


def exps_block(rows):
    place = lax.broadcasted_iota(I32, (16, T), 0)
    out = jnp.zeros((16, T), F32)
    for r, e in enumerate(rows):
        out = jnp.where(place == r, e, out)
    return out.astype(I32).astype(I16)


def main_kernel(slots, counts, meta, x_ref, mine_ref, other_ref, col_ref, r_ref, dr_ref,
                send_ref, keep_row_ref, keep_core_ref, colt_ref, gram_ref,
                core_acc, gram_acc, rows_s, exps):
    h = pl.program_id(0)
    q = pl.program_id(1)
    c = meta[0]
    span = q * 2 + jnp.where(h == 0, c, 1 - c)

    @pl.when((h == 0) & (q == 0))
    def _():
        core_acc[...] = jnp.zeros_like(core_acc)
        gram_acc[...] = jnp.zeros_like(gram_acc)
        colt_ref[...] = jnp.zeros_like(colt_ref)
        exps[...] = jnp.zeros_like(exps)

    @pl.when(h == 0)
    def _():
        rows_s[...] = mine_ref[0]

    @pl.when(h == 1)
    def _():
        rows_s[...] = other_ref[0]

    rows = rows_s[...]
    rows_t = rows.T
    lhs_core = jnp.concatenate([rows_t[T:], rows_t[:T]], axis=1)
    gram_acc[...] += jnp.dot(rows_t[T:], rows, preferred_element_type=F32)
    total = None
    for s in range(SC):
        live = s < counts[span]
        base = (span * SC + s) * 3
        k = slots[base]
        b = slots[base + 2]
        x = x_ref[0, 0, 0, s]
        x = jnp.where(live, x, jnp.zeros_like(x))
        near = jnp.dot(x, col_ref[b], preferred_element_type=F32).astype(BF16)
        far = lax.dot_general(x, rows, TN, preferred_element_type=F32).astype(BF16)
        r = r_ref[k]
        dr = dr_ref[k]
        row_term = lax.dot_general(near, jnp.concatenate([r, dr], axis=1), NT, preferred_element_type=F32)
        total = row_term if total is None else total + row_term
        colt_ref[b] += jnp.dot(far, jnp.concatenate([r, dr], axis=0), preferred_element_type=F32)
        place = pl.ds(pl.multiple_of(k * T, T), T)
        core_acc[place] += jnp.dot(lhs_core, jnp.concatenate([near[:, :T], near[:, T:]], axis=0),
                                   preferred_element_type=F32)

    @pl.when(h == 0)
    def _():
        keep_row_ref[q] = total

    @pl.when(h == 1)
    def _():
        val, e = enc(total)
        send_ref[pl.ds(pl.multiple_of(q * T, T), T)] = val
        exps[pl.ds(q, 1)] = e

    @pl.when((h == 1) & (q == NQ - 1))
    def _():
        keep_core_ref[...] = core_acc[pl.ds(pl.multiple_of(c * HALF, HALF), HALF)]
        start = (1 - c) * HALF

        def body(g, carry):
            val, e = enc(core_acc[pl.ds(pl.multiple_of(start + g * GRP, 32), GRP)])
            send_ref[pl.ds(pl.multiple_of(SEND_CORE + g * GRP, 32), GRP)] = val
            exps[pl.ds(NQ + g, 1)] = e
            return carry

        lax.fori_loop(0, NGRP, body, 0)
        send_ref[SEND_EXP:] = exps[...].astype(I32).astype(I16)
        part = gram_acc[pl.ds(pl.multiple_of(meta[1] * 8, 8), 8)]
        gram_ref[0:8] = part[:, :T]
        gram_ref[8:16] = part[:, T:]


def merge_kernel(recv_ref, keep_core_ref, colt_ref, gram_ref, out_ref):
    exps = exps_of(recv_ref[SEND_EXP:])
    g_hi, g_lo, g_e = enc_wide(gram_ref[...])
    for i in range(NR):
        val, e0 = enc(colt_ref[i])
        out_ref[i, 0:T] = val
        rows = [e0]
        for j in range(PART // GRP):
            g = i * (PART // GRP) + j
            got = dec(recv_ref[SEND_CORE + g * GRP:SEND_CORE + (g + 1) * GRP], exps[NQ + g:NQ + g + 1])
            val, e = enc(got + keep_core_ref[g * GRP:(g + 1) * GRP])
            out_ref[i, C1_CORE + j * GRP:C1_CORE + (j + 1) * GRP] = val
            rows.append(e)
        out_ref[i, C1_GRAM:C1_GRAM + 16] = g_hi
        out_ref[i, C1_GRAM + 16:C1_GRAM + 32] = g_lo
        rows.append(g_e)
        out_ref[i, C1_EXP:C1_ROWS] = exps_block(rows)


def second_kernel(r1_ref, recv_ref, keep_row_ref, out_ref, cols_ref, core_s):
    col = jnp.zeros((T, T), F32)
    gram = jnp.zeros((16, T), F32)
    core = [jnp.zeros((GRP, T), F32) for _ in range(PART // GRP)]
    all_e = [exps_of(r1_ref[i, C1_EXP:C1_ROWS]) for i in range(NR)]
    for i in range(NR):
        e = all_e[i]
        col = col + dec(r1_ref[i, 0:T], e[0:1])
        gram = gram + dec_wide(r1_ref[i, C1_GRAM:C1_GRAM + 16], r1_ref[i, C1_GRAM + 16:C1_GRAM + 32], e[4:5])
    cols_ref[...] = col
    for j in range(PART // GRP):
        acc = jnp.zeros((GRP, T), F32)
        for i in range(NR):
            acc = acc + dec(r1_ref[i, C1_CORE + j * GRP:C1_CORE + (j + 1) * GRP], all_e[i][1 + j:2 + j])
        core_s[j * GRP:(j + 1) * GRP] = acc
    core_s[PART:] = jnp.zeros((PIECE, T), F32)
    exps = exps_of(recv_ref[SEND_EXP:])
    g_hi, g_lo, g_e = enc_wide(gram)
    for q in range(NQ):
        got = dec(recv_ref[q * T:(q + 1) * T], exps[q:q + 1])
        val, e0 = enc(got + keep_row_ref[q])
        out_ref[q, 0:T] = val
        val, e1 = enc(core_s[q * PIECE:(q + 1) * PIECE])
        out_ref[q, C2_CORE:C2_CORE + PIECE] = val
        out_ref[q, C2_GRAM:C2_GRAM + 16] = g_hi
        out_ref[q, C2_GRAM + 16:C2_GRAM + 32] = g_lo
        out_ref[q, C2_EXP:C2_ROWS] = exps_block([e0, e1, g_e])


def third_kernel(meta, r2_ref, cols_ref, r_ref, dr_ref, hv_ref, out_ref, gram_s, cross_s):
    total = cols_ref[...]
    core = jnp.zeros((PIECE, T), F32)
    for q in range(NQ):
        e = exps_of(r2_ref[q, C2_EXP:C2_ROWS])
        total = total + dec(r2_ref[q, 0:T], e[0:1])
        core = core + dec(r2_ref[q, C2_CORE:C2_CORE + PIECE], e[1:2])
        g = dec_wide(r2_ref[q, C2_GRAM:C2_GRAM + 16], r2_ref[q, C2_GRAM + 16:C2_GRAM + 32], e[2:3])
        cross_s[q * 8:(q + 1) * 8] = g[0:8]
        gram_s[q * 8:(q + 1) * 8] = g[8:16]
    hv_ref[...] = (-total).astype(BF16)
    gram = gram_s[...]
    cross = cross_s[...]
    cross_s[...] = cross + cross.T
    d_gram = cross_s[...]
    r = r_ref[0].astype(F32)
    dr = dr_ref[0].astype(F32)
    rows = pl.ds(pl.multiple_of(meta[3], PIECE), PIECE)
    g_rows = gram_s[rows]
    d_rows = cross_s[rows]
    mm = lambda a, b: jnp.dot(a, b, precision=HIGH, preferred_element_type=F32)
    left = mm(d_rows, r) + mm(g_rows, dr)
    right = mm(g_rows, r)
    piece = mm(left, gram) + mm(right, d_gram) - core
    val, e = enc(piece)
    block = exps_block([e])
    for q in range(NQ):
        out_ref[q, 0:PIECE] = val
        out_ref[q, PIECE:P3_ROWS] = block


def fourth_kernel(r3_ref, out_ref):
    place = lax.broadcasted_iota(I32, (16, T), 0)
    exps = jnp.zeros((16, T), F32)
    for q in range(NQ - 1):
        exps = jnp.where(place == q, exps_of(r3_ref[q, PIECE:P3_ROWS])[0:1], exps)
    exps = exps.astype(I32).astype(I16)
    for i in range(NR):
        for q in range(NQ - 1):
            out_ref[i, q * PIECE:(q + 1) * PIECE] = r3_ref[q, 0:PIECE]
        out_ref[i, PART:P4_ROWS] = exps


def last_kernel(meta, mine_ref, other_ref, out_ref):
    h = pl.program_id(0)

    def put(ref):
        e = exps_of(ref[0, PART:P4_ROWS])
        for q in range(NQ - 1):
            out_ref[q * PIECE:(q + 1) * PIECE] = dec(ref[0, q * PIECE:(q + 1) * PIECE], e[q:q + 1])

    @pl.when(h == 0)
    def _():
        put(mine_ref)

    @pl.when(h == 1)
    def _():
        put(other_ref)


def shape(*dims, dtype=F32):
    return jax.ShapeDtypeStruct(dims, dtype)


WHOLE = pl.BlockSpec(memory_space=pltpu.VMEM)
BIG = pltpu.CompilerParams(vmem_limit_bytes=48 * 1024 * 1024)


def per_device(tile_values, tile_slots, counts, factor, d_factor, core_rel, d_core):
    swap = lambda a: lax.ppermute(a, "core", [(0, 1), (1, 0)])
    zx = lax.axis_index("z") * 2 + lax.axis_index("xh")
    row = lax.axis_index("xl") * 4 + lax.axis_index("y")
    core = lax.axis_index("core")
    first = core * HALF + row * PART + zx * PIECE
    meta = jnp.stack([core, zx, jnp.minimum(first // T, RELS - 1), first % T]).astype(I32)

    pair = jnp.concatenate([d_factor, factor], axis=1)
    mine = lax.all_to_all(jnp.broadcast_to(pair[None], (NQ, T, 2 * T)), ("z", "xh"), 0, 0, tiled=True)
    other = swap(mine)
    columns = lax.all_to_all(jnp.broadcast_to(pair[None], (NR, T, 2 * T)), ("xl", "y"), 0, 0, tiled=True)

    span_of = lambda h, q, m: q * 2 + jnp.where(h == 0, m[0], 1 - m[0])
    send, keep_row, keep_core, colt, gram = pl.pallas_call(
        main_kernel,
        grid_spec=pltpu.PrefetchScalarGridSpec(
            num_scalar_prefetch=3,
            grid=(2, NQ),
            in_specs=[
                pl.BlockSpec((1, 1, 1, SC, T, T), lambda h, q, s, n, m: (0, 0, span_of(h, q, m), 0, 0, 0)),
                pl.BlockSpec((1, T, 2 * T), lambda h, q, s, n, m: (jnp.where(h == 0, q, NQ - 1), 0, 0)),
                pl.BlockSpec((1, T, 2 * T), lambda h, q, s, n, m: (jnp.where(h == 0, 0, q), 0, 0)),
                WHOLE, WHOLE, WHOLE,
            ],
            out_specs=[WHOLE] * 5,
            scratch_shapes=[
                pltpu.VMEM((RELS * T, T), F32),
                pltpu.VMEM((T, 2 * T), F32),
                pltpu.VMEM((T, 2 * T), BF16),
                pltpu.VMEM((48, T), F32),
            ],
        ),
        out_shape=[shape(SEND_ROWS, T, dtype=I16), shape(NQ, T, T), shape(HALF, T), shape(NR, T, T), shape(16, T)],
        compiler_params=BIG,
    )(tile_slots.reshape(-1), counts.reshape(-1), meta, tile_values, mine, other, columns, core_rel, d_core)

    recv = swap(send)
    c1 = pl.pallas_call(
        merge_kernel,
        in_specs=[WHOLE] * 4, out_specs=WHOLE,
        out_shape=shape(NR, C1_ROWS, T, dtype=I16), compiler_params=BIG,
    )(recv, keep_core, colt, gram)
    r1 = lax.all_to_all(c1, ("xl", "y"), 0, 0, tiled=True)
    c2, cols = pl.pallas_call(
        second_kernel,
        in_specs=[WHOLE] * 3, out_specs=[WHOLE] * 2,
        out_shape=[shape(NQ, C2_ROWS, T, dtype=I16), shape(T, T)],
        scratch_shapes=[pltpu.VMEM((PART + PIECE, T), F32)], compiler_params=BIG,
    )(r1, recv, keep_row)
    r2 = lax.all_to_all(c2, ("z", "xh"), 0, 0, tiled=True)
    hv_factor, c3 = pl.pallas_call(
        third_kernel,
        grid_spec=pltpu.PrefetchScalarGridSpec(
            num_scalar_prefetch=1,
            grid=(1,),
            in_specs=[
                WHOLE, WHOLE,
                pl.BlockSpec((1, T, T), lambda i, m: (m[2], 0, 0)),
                pl.BlockSpec((1, T, T), lambda i, m: (m[2], 0, 0)),
            ],
            out_specs=[WHOLE, WHOLE],
            scratch_shapes=[pltpu.VMEM((T, T), F32), pltpu.VMEM((T, T), F32)],
        ),
        out_shape=[shape(T, T, dtype=BF16), shape(NQ, P3_ROWS, T, dtype=I16)],
        compiler_params=BIG,
    )(meta, r2, cols, core_rel, d_core)
    r3 = lax.all_to_all(c3, ("z", "xh"), 0, 0, tiled=True)
    c4 = pl.pallas_call(
        fourth_kernel,
        in_specs=[WHOLE], out_specs=WHOLE,
        out_shape=shape(NR, P4_ROWS, T, dtype=I16), compiler_params=BIG,
    )(r3)
    r4 = lax.all_to_all(c4, ("xl", "y"), 0, 0, tiled=True)
    r5 = swap(r4)
    hv_core = pl.pallas_call(
        last_kernel,
        grid_spec=pltpu.PrefetchScalarGridSpec(
            num_scalar_prefetch=1,
            grid=(2, NR),
            in_specs=[
                pl.BlockSpec((1, P4_ROWS, T), lambda h, i, m: (jnp.where(h == 0, i, NR - 1), 0, 0)),
                pl.BlockSpec((1, P4_ROWS, T), lambda h, i, m: (jnp.where(h == 0, 0, i), 0, 0)),
            ],
            out_specs=pl.BlockSpec((PART, T), lambda h, i, m: (jnp.where(h == 0, m[0], 1 - m[0]) * NR + i, 0)),
        ),
        out_shape=shape(RELS * T, T), compiler_params=BIG,
    )(meta, r4, r5)
    return hv_factor, hv_core.reshape(RELS, T, T)


def solution(mesh):
    chips = Mesh(mesh.devices.reshape(2, 4, 8, 2, 2), ("xl", "y", "z", "xh", "core"))
    row, col = ("xl", "y"), ("z", "xh", "core")
    placed = (
        P(row, col, None, None, None, None),
        P(row, col, None, None, None),
        P(row, col, None),
        P(row + col, None),
        P(row + col, None),
        P(),
        P(),
    )
    return jax.shard_map(
        per_device,
        mesh=chips,
        in_specs=placed,
        out_specs=(P(row + col, None), P()),
        check_vma=False,
    )
```

time: 567 us -> 194 us (0.34); the launches traced: 556 us -> 190 us
  waiting for transfers between devices: 371 us -> 14.8 us
  matrix products: 101 us -> 0 us
  blocking collectives: 29.1 us -> 121 us
  Pallas kernels: 0 us -> 42.9 us
  local copies, waits for them, and re-layouts: 35.2 us -> 4.31 us
  between operations: 14.5 us -> 0.7 us
  starting transfers between devices: 0.16 us -> 5.94 us
    psum x1 -> x0, waiting for transfers between devices: 274 us -> none  [per_device(): core_sum = lax.psum(core_local, ('row', 'col'))]
    all_to_all x0 -> x5, blocking collectives: none -> 121 us  [the longest x1 39.8 us: per_device(): lax.all_to_all(jnp.broadcast_to(pair[None], (NQ, T, 2 * T)), ('z', 'xh'),...]
    dot_general x18 -> x0, matrix products: 101 us -> none  [the longest x1 21.9 us: per_device(): jnp.einsum('sk,svd->kvd', col_onehot, col_term, precision=HIGH)]
    reduce_scatter x2 -> x0, waiting for transfers between devices: 91.8 us -> none  [the longest x1 50.8 us: per_device(): lax.psum_scatter(row_place, 'col', scatter_dimension=0, tiled=True)]
    pallas_call x0 -> x6, Pallas kernels: none -> 42.9 us  [the longest x1 32.8 us: per_device(): pl.pallas_call(main_kernel, grid_spec=pltpu.PrefetchScalarGridSpec(num_sc...]
    all_gather x1 -> x0, blocking collectives: 29.1 us -> none  [per_device(): column_block = lax.all_gather(pair, 'row', axis=0, tiled=True)]
    gather x4 -> x0, local copies, waits for them, and re-layouts: 20.6 us -> none  [the longest x1 7.78 us: per_device(): rows_fac = jnp.take(row_tiles, group_ids * per_span + index[:, 1], axis=0)]
    all_to_all x0 -> x1, waiting for transfers between devices: none -> 8.9 us  [per_device(): lax.all_to_all(jnp.broadcast_to(pair[None], (NR, T, 2 * T)), ('xl', 'y'),...]
  transfers between devices with their start and end apart: 4 -> 4, of which waited for: 4 -> 3; matrix products, arithmetic and copies ran while one was open for 21% -> 1% of each run, Pallas kernels for 0% -> 0%
where the time goes in v1:
time: 194 us; the launch traced here: 190 us
  blocking collectives  121 us (62%)
  Pallas kernels  42.9 us (22%)
  waiting for transfers between devices  14.8 us (8%)
  starting transfers between devices  5.94 us (3%)
  local copies, waits for them, and re-layouts  4.31 us (2%)
    all_to_all x1, blocking collectives, per_device(): lax.all_to_all(jnp.broadcast_to(pair[None], (NQ, T, 2 * T)), ('z', 'xh'),...  39.8 us
    pallas_call x1, Pallas kernels, per_device(): pl.pallas_call(main_kernel, grid_spec=pltpu.PrefetchScalarGridSpec(num_sc...  32.8 us
    all_to_all x1, blocking collectives, per_device(): r2 = lax.all_to_all(c2, ('z', 'xh'), 0, 0, tiled=True)  28.2 us
    all_to_all x1, blocking collectives, per_device(): r1 = lax.all_to_all(c1, ('xl', 'y'), 0, 0, tiled=True)  21.9 us
    all_to_all x1, blocking collectives, per_device(): r4 = lax.all_to_all(c4, ('xl', 'y'), 0, 0, tiled=True)  17 us
    all_to_all x1, blocking collectives, per_device(): r3 = lax.all_to_all(c3, ('z', 'xh'), 0, 0, tiled=True)  14.3 us
    all_to_all x1, waiting for transfers between devices, per_device(): lax.all_to_all(jnp.broadcast_to(pair[None], (NR, T, 2 * T)), ('xl', 'y'),...  8.9 us
    pallas_call x1, Pallas kernels, per_device(): pl.pallas_call(last_kernel, grid_spec=pltpu.PrefetchScalarGridSpec(num_sc...  6.48 us
  transfers between devices with their start and end apart: 4, of which 3 were waited for; matrix products, arithmetic and copies ran while one was open for 1% of the time, Pallas kernels for 0%

profile of v1, /device:TPU:2, one launch (start us, length us, event | category | flops | bytes accessed | tf_op | source)
XLA Modules:
  0.0 190.0 jit_solution(927756452056499411)
XLA Ops:
  0.6 0.8 constant_dynamic-update-slice_fusion.1
  1.4 0.8 constant_dynamic-update-slice_fusion
  2.2 0.1 broadcast_in_dim.4
  2.3 0.0 copy-start.3
  2.3 39.8 %all_to_all.30.mine_ref = bf16[16,128,256]{2,1,0:T(8,128)(2,1)S(1)} all-to-all(bf16[16,128,256]{2,1,0:T(8,128)(2,1)S(1)} %broadcast_in_dim.4), channel_id=1, replica_groups=mesh['xl'=2,'y'=4,'z'=8,'xh'=2,'core'=2] {'z','xh'}, dimensions={0} | all-to-all | bytes 2097152 | tf_op jit(solution)/shard_map/all_to_all | solution.py:286
  42.1 0.8 broadcast_in_dim.5
  43.0 5.9 %all-to-all-start.1 = ((bf16[8,128,256]{2,1,0:T(8,128)(2,1)}), bf16[8,128,256]{2,1,0:T(8,128)(2,1)S(1)}, u32[]{:S(2)}, u32[]{:S(2)}) async-start(bf16[8,128,256]{2,1,0:T(8,128)(2,1)} %broadcast_in_dim.5), calls=%async_computation.1 | async-start | bytes 1048576 | tf_op jit(solution)/shard_map/all_to_all | solution.py:288
  48.9 0.1 copy.9
  49.0 0.2 reshape.14.slots
  49.2 0.1 pad_add_fusion.meta
  49.3 8.9 %all-to-all-done.1.col_ref = bf16[8,128,256]{2,1,0:T(8,128)(2,1)S(1)} async-done(((bf16[8,128,256]{2,1,0:T(8,128)(2,1)}), bf16[8,128,256]{2,1,0:T(8,128)(2,1)S(1)}, u32[]{:S(2)}, u32[]{:S(2)}) %all-to-all-start.1) | async-done | bytes 524320 | tf_op jit(solution)/shard_map/all_to_all | solution.py:288
  58.2 32.8 %shard_map.86 = (s16[5936,128]{1,0:T(8,128)(2,1)S(1)}, f32[16,128,128]{2,1,0:T(8,128)S(1)}, f32[3840,128]{1,0:T(8,128)}, f32[8,128,128]{2,1,0:T(8,128)S(1)}, f32[16,128]{1,0:T(8,128)S(1)}) custom-call(s32[288]{0:T(512)S(1)} %reshape.14.slots, s32[32]{0:T(128)S(1)} %bitcast.6, s32[4]{0:T(128)S(1)} %pad_add_fusion.meta, ...), custom_call_target="tpu_custom_call" | custom-call | tf_op jit(solution)/shard_map/pallas_call | solution.py:291
  91.0 3.3 %collective-permute-done.1.recv_ref = s16[5936,128]{1,0:T(8,128)(2,1)S(1)} collective-permute-done((s16[5936,128]{1,0:T(8,128)(2,1)S(1)}, s16[5936,128]{1,0:T(8,128)(2,1)S(1)}, u32[]{:S(2)}, u32[]{:S(2)}) %collective-permute-start.1) | collective-permute-done | bytes 1519648 | tf_op jit(solution)/shard_map/ppermute | solution.py:278
  94.3 1.5 copy-done.2
  95.9 0.8 shard_map.87
  96.6 21.9 %all_to_all.31.r1_ref = s16[8,656,128]{2,1,0:T(8,128)(2,1)S(1)} all-to-all(s16[8,656,128]{2,1,0:T(8,128)(2,1)S(1)} %shard_map.87), channel_id=1, replica_groups=mesh['xl'=2,'y'=4,'z'=8,'xh'=2,'core'=2] {'xl','y'}, dimensions={0} | all-to-all | bytes 2686976 | tf_op jit(solution)/shard_map/all_to_all | solution.py:320
  118.5 0.8 shard_map.88
  119.3 28.2 %all_to_all.32.r2_ref = s16[16,208,128]{2,1,0:T(8,128)(2,1)S(1)} all-to-all(s16[16,208,128]{2,1,0:T(8,128)(2,1)S(1)} %get-tuple-element.16), channel_id=1, replica_groups=mesh['xl'=2,'y'=4,'z'=8,'xh'=2,'core'=2] {'z','xh'}, dimensions={0} | all-to-all | bytes 1703936 | tf_op jit(solution)/shard_map/all_to_all | solution.py:327
  147.6 2.0 %shard_map.89 = (bf16[128,128]{1,0:T(8,128)(2,1)}, s16[16,48,128]{2,1,0:T(8,128)(2,1)S(1)}) custom-call(s32[4]{0:T(128)S(1)} %pad_add_fusion.meta, s16[16,208,128]{2,1,0:T(8,128)(2,1)S(1)} %all_to_all.32.r2_ref, f32[128,128]{1,0:T(8,128)S(1)} %get-tuple-element.17.cols_ref, bf16[60,128,128]{2,1,0:T(8,128)(2,1)S(1)} %copy-done, ...), custom_call_target="tpu_custom_call" | custom-call | tf_op jit(solution)/shard_map/pallas_call | solution.py:328
  149.5 14.3 %all_to_all.33.r3_ref = s16[16,48,128]{2,1,0:T(8,128)(2,1)S(1)} all-to-all(s16[16,48,128]{2,1,0:T(8,128)(2,1)S(1)} %get-tuple-element.19), channel_id=1, replica_groups=mesh['xl'=2,'y'=4,'z'=8,'xh'=2,'core'=2] {'z','xh'}, dimensions={0} | all-to-all | bytes 393216 | tf_op jit(solution)/shard_map/all_to_all | solution.py:344
  163.8 0.1 shard_map.90
  164.0 17.0 %all_to_all.34.mine_ref = s16[8,496,128]{2,1,0:T(8,128)(2,1)S(1)} all-to-all(s16[8,496,128]{2,1,0:T(8,128)(2,1)S(1)} %shard_map.90), channel_id=1, replica_groups=mesh['xl'=2,'y'=4,'z'=8,'xh'=2,'core'=2] {'xl','y'}, dimensions={0} | all-to-all | bytes 2031616 | tf_op jit(solution)/shard_map/all_to_all | solution.py:350
  181.0 2.6 %collective-permute-done.2.other_ref = s16[8,496,128]{2,1,0:T(8,128)(2,1)S(1)} collective-permute-done((s16[8,496,128]{2,1,0:T(8,128)(2,1)S(1)}, s16[8,496,128]{2,1,0:T(8,128)(2,1)S(1)}, u32[]{:S(2)}, u32[]{:S(2)}) %collective-permute-start.2) | collective-permute-done | bytes 1015840 | tf_op jit(solution)/shard_map/ppermute | solution.py:278
  183.6 6.5 %shard_map.91 = f32[7680,128]{1,0:T(8,128)} custom-call(s32[4]{0:T(128)S(1)} %pad_add_fusion.meta, s16[8,496,128]{2,1,0:T(8,128)(2,1)S(1)} %all_to_all.34.mine_ref, s16[8,496,128]{2,1,0:T(8,128)(2,1)S(1)} %collective-permute-done.2.other_ref), custom_call_target="tpu_custom_call" | custom-call | tf_op jit(solution)/shard_map/pallas_call | solution.py:352
  (12 shorter events, 0.0 us)
Async XLA Ops:
  2.3 46.6 %copy-start.4 = (s32[1,1,32,3,3]{2,1,4,3,0:T(1,128)S(1)}, s32[1,1,32,3,3]{2,1,4,3,0:T(1,128)}, u32[]{:S(2)}) copy-start(s32[1,1,32,3,3]{2,1,4,3,0:T(1,128)} %param.8) | copy-start | bytes 3460
  2.3 55.9 %copy-start.3 = (s32[1,1,32]{2,1,0:T(1,128)S(1)}, s32[1,1,32]{2,1,0:T(1,128)}, u32[]{:S(2)}) copy-start(s32[1,1,32]{2,1,0:T(1,128)} %param.9) | copy-start | bytes 388
  42.1 16.1 %collective-permute-start = (bf16[16,128,256]{2,1,0:T(8,128)(2,1)S(1)}, bf16[16,128,256]{2,1,0:T(8,128)(2,1)S(1)}, u32[]{:S(2)}, u32[]{:S(2)}) collective-permute-start(bf16[16,128,256]{2,1,0:T(8,128)(2,1)S(1)} %all_to_all.30.mine_ref), channel_id=1, source_target_pairs={{0,1},{1,0},{2,3},{3,2},{4,5},{5,4},{6,7},{7,6},{8,9},{9,8},{10,11... | collective-permute-start | bytes 3145736 | tf_op jit(solution)/shard_map/ppermute | solution.py:278
  43.0 15.2 %all-to-all-start.1 = ((bf16[8,128,256]{2,1,0:T(8,128)(2,1)}), bf16[8,128,256]{2,1,0:T(8,128)(2,1)S(1)}, u32[]{:S(2)}, u32[]{:S(2)}) async-start(bf16[8,128,256]{2,1,0:T(8,128)(2,1)} %broadcast_in_dim.5), calls=%async_computation.1 | async-start | bytes 1048576 | tf_op jit(solution)/shard_map/all_to_all | solution.py:288
  91.0 3.3 %collective-permute-start.1 = (s16[5936,128]{1,0:T(8,128)(2,1)S(1)}, s16[5936,128]{1,0:T(8,128)(2,1)S(1)}, u32[]{:S(2)}, u32[]{:S(2)}) collective-permute-start(s16[5936,128]{1,0:T(8,128)(2,1)S(1)} %get-tuple-element.11), channel_id=1, source_target_pairs={{0,1},{1,0},{2,3},{3,2},{4,5},{5,4},{6,7},{7,6},{8,9},{9,8},{10,11... | collective-permute-start | bytes 4558856 | tf_op jit(solution)/shard_map/ppermute | solution.py:278
  94.3 1.5 copy-start.2
  118.5 29.0 %copy-start = (bf16[60,128,128]{2,1,0:T(8,128)(2,1)S(1)}, bf16[60,128,128]{2,1,0:T(8,128)(2,1)}, u32[]{:S(2)}) copy-start(bf16[60,128,128]{2,1,0:T(8,128)(2,1)} %r_ref.3) | copy-start | bytes 5898244
  118.5 29.0 %copy-start.1 = (bf16[60,128,128]{2,1,0:T(8,128)(2,1)S(1)}, bf16[60,128,128]{2,1,0:T(8,128)(2,1)}, u32[]{:S(2)}) copy-start(bf16[60,128,128]{2,1,0:T(8,128)(2,1)} %dr_ref.3) | copy-start | bytes 5898244
  180.9 2.6 %collective-permute-start.2 = (s16[8,496,128]{2,1,0:T(8,128)(2,1)S(1)}, s16[8,496,128]{2,1,0:T(8,128)(2,1)S(1)}, u32[]{:S(2)}, u32[]{:S(2)}) collective-permute-start(s16[8,496,128]{2,1,0:T(8,128)(2,1)S(1)} %all_to_all.34.mine_ref), channel_id=1, source_target_pairs={{0,1},{1,0},{2,3},{3,2},{4,5},{5,4},{6,7},{7,6},{8,9},{9,8},{10,11... | collective-permute-start | bytes 3047432 | tf_op jit(solution)/shard_map/ppermute | solution.py:278
